TPU v7x, 256 devices: a whole 4x4x8 slice. The times are simulated.
256 devices in a mesh: dp: 4 (over x_lo, core), col: 64 (over y, z, x_hi).
Axes of the slice: x: 4 (x_hi: 2, x_lo: 2; x = x_hi * 2 + x_lo), y: 4, z: 8, core: 2. Of those that a mesh axis runs over, the one named last changes fastest.
Arguments:
- proj: bfloat16 [8192, 2048], P('col', 'dp'), may hold values from -0.0625 to 0.0625
- mean: float32 [8192], P('col'), may hold values from -0.75 to 0.75
- root: bfloat16 [8192, 8192], P(None, 'col'), may hold values from -0.1875 to 0.1875
- resid_var: float32 [2048], P('dp'), may hold values from 0.05 to 1
- targets: float32 [65536], replicated, may hold values from -8 to 8
- indices: int32 [2048], P('dp'), may hold values from 0 to 65535
Outputs:
- grad_mean: float32 [8192], P('col')
- grad_root: float32 [8192, 8192], P('dp', 'col')
- grad_proj: float32 [8192, 2048], P('col', 'dp')
All inputs are finite; a program needn't handle non-finite values.
Results may differ from a plain program's by a relative error of at most 0.0026.
Values may be sent and summed in bfloat16 or wider, within the bound.
A program may use at most 64 MiB of HBM per device.

v0:
```python
import jax
import jax.numpy as jnp
import numpy as np
from jax import lax
from jax.sharding import PartitionSpec as P

WINDOW = 65536


freedom = 4.0
half_knots = [
    0.2453407083009012,
    0.7374737285453944,
    1.234076215395323,
    1.7385377121165861,
    2.2549740020892757,
    2.7888060584281305,
    3.3478545673832163,
    3.944764040115625,
    4.603682449550744,
    5.387480890011233,
]
half_weights = [
    0.4622436696006101,
    0.2866755053628341,
    0.1090172060200233,
    0.024810520887463612,
    0.0032437733422378567,
    0.00022833863601635319,
    7.802556478532063e-06,
    1.0860693707692819e-07,
    4.3993409922731804e-10,
    2.2293936455341508e-13,
]


def hermite_table():
    positive = np.array(half_knots)
    heights = np.array(half_weights)
    knots = np.concatenate([-positive[::-1], positive])
    weights = np.concatenate([heights[::-1], heights])
    return (knots, weights)


def expected_slopes(observed, post_mean, post_var, factor):
    knots, weights = hermite_table()
    knots = jnp.asarray(knots, jnp.float32)[:, None]
    weights = jnp.asarray(weights / np.sqrt(np.pi), jnp.float32)[:, None]
    spread_root = jnp.sqrt(2.0 * post_var)
    values = post_mean[None, :] + spread_root[None, :] * knots
    gap = observed[None, :] - values
    slope = (freedom + 1.0) * gap / (freedom + gap * gap)
    slope_mean = factor * jnp.sum(weights * slope, axis=0)
    slope_var = factor * jnp.sum(weights * slope * knots, axis=0) / spread_root
    return (slope_mean, slope_var)


def on_device(proj, mean, root, resid_var, targets, indices):
    group_rows = proj.shape[1]
    whole = lax.all_gather(proj, "col", axis=0, tiled=True)
    latent = lax.dot_general(
        root, whole, (((0,), (0,)), ((), ())), preferred_element_type=jnp.float32
    )
    squares = jnp.sum(latent * latent, axis=0)
    partial_mean = jnp.dot(
        mean, proj, precision=lax.Precision.HIGHEST, preferred_element_type=jnp.float32
    )
    post_mean, square_sum = lax.psum((partial_mean, squares), "col")
    post_var = resid_var + square_sum
    observed = jnp.take(targets, indices)
    factor = WINDOW / (group_rows * lax.axis_size("dp"))
    slope_mean, slope_var = expected_slopes(observed, post_mean, post_var, factor)
    weighted = (2.0 * slope_var[None, :] * latent).astype(jnp.bfloat16)
    mean_part = jnp.dot(
        proj, slope_mean, precision=lax.Precision.HIGHEST, preferred_element_type=jnp.float32
    )
    grad_mean = lax.psum(mean_part, "dp")
    grad_root = lax.psum_scatter(
        lax.dot_general(
            whole, weighted, (((1,), (1,)), ((), ())), preferred_element_type=jnp.float32
        ),
        "dp",
        scatter_dimension=0,
        tiled=True,
    )
    summed = lax.psum_scatter(
        jnp.dot(root, weighted, preferred_element_type=jnp.float32),
        "col",
        scatter_dimension=0,
        tiled=True,
    )
    grad_proj = mean[:, None] * slope_mean[None, :] + summed
    return (grad_mean, grad_root, grad_proj)


def solution(mesh):
    return jax.shard_map(
        on_device,
        mesh=mesh,
        in_specs=(P("col", "dp"), P("col"), P(None, "col"), P("dp"), P(), P("dp")),
        out_specs=(P("col"), P("dp", "col"), P("col", "dp")),
        check_vma=False,
    )
```

profile of v0, /device:TPU:0, one launch (start us, length us, event | category | flops | bytes accessed | tf_op | source)
XLA Modules:
  0.0 813.7 jit_solution(17693407083442354464)
XLA Ops:
  7.2 0.0 copy-start
  7.2 0.0 all-gather.2.cloned.1.call-start
  7.2 0.7 all-gather.2.cloned.1.call-update
  7.9 0.0 reduce-scatter.3.cloned.1.call-start
  8.0 0.7 compare_select_fusion
  8.7 3.6 gather_fusion
  12.3 0.7 and_select_fusion
  13.0 1.1 fusion.2
  14.1 0.0 copy-start.3
  14.1 0.0 copy-start.4
  14.1 149.2 %all-gather.2.cloned.1.call-done = bf16[8192,512]{1,0:T(8,128)(2,1)} async-done(((bf16[128,512]{1,0:T(8,128)(2,1)}), bf16[8192,512]{1,0:T(8,128)(2,1)}) %all-gather.2.cloned.1.call-update) | async-done | bytes 8388624 | tf_op jit(solution)/shard_map/all_gather | solution.py:60
  163.3 0.0 copy-done
  163.3 4.7 multiply_reduce_fusion
  168.0 180.5 %all-reduce = (f32[512]{0:T(512)S(1)}, f32[512]{0:T(512)S(1)}) all-reduce(f32[512]{0:T(512)S(1)} %get-tuple-element.16, f32[512]{0:T(512)S(1)} %bitcast.19), channel_id=1, replica_groups=mesh['dp'=4,'col'=64] {'col'}, use_global_device_ids=true, to_apply=%region_2.0 | all-reduce | flops 1024 | bytes 8192 | tf_op jit(solution)/shard_map/psum | solution.py:68
  348.5 0.0 copy-done.3
  348.5 0.0 copy-done.4
  348.5 0.0 copy-done.5
  348.5 0.1 multiply_reduce_fusion.1
  348.6 8.1 convolution_bitcast_fusion.1
  356.7 0.0 reduce-scatter.3.cloned.1.call-update
  356.7 0.0 reduce-scatter.5.cloned.1.call-start
  356.8 8.7 %convolution_bitcast_fusion = f32[8192,512]{0,1:T(8,128)} fusion(bf16[8192,128]{1,0:T(8,128)(2,1)S(1)} %copy-done, f32[128,512]{1,0:T(8,128)S(1)} %get-tuple-element.17, f32[512]{0:T(512)S(1)} %fusion.1), kind=kOutput, calls=%fused_computation.1 | convolution fusion | flops 1073872896 | bytes 19138560 | tf_op jit(solution)/shard_map/dot_general | solution.py:87
  365.5 0.0 reduce-scatter.5.cloned.1.call-update
  365.6 0.9 copy-done.1
  366.4 0.1 convolution_bitcast_fusion.2
  366.6 6.7 psum.23
  373.3 23.8 %reduce-scatter.3.cloned.1.call-done = f32[2048,128]{0,1:T(8,128)} async-done(((f32[8192,128]{0,1:T(8,128)}), f32[2048,128]{0,1:T(8,128)}) %reduce-scatter.3.cloned.1.call-update) | async-done | bytes 1048592 | tf_op jit(solution)/shard_map/reduce_scatter | solution.py:78
  397.1 2.5 copy.15
  399.6 405.6 %reduce-scatter.5.cloned.1.call-done = f32[128,512]{0,1:T(8,128)} async-done(((f32[8192,512]{0,1:T(8,128)}), f32[128,512]{0,1:T(8,128)}) %reduce-scatter.5.cloned.1.call-update) | async-done | bytes 262160 | tf_op jit(solution)/shard_map/reduce_scatter | solution.py:86
  805.2 0.0 copy-done.2
  805.2 1.1 multiply_add_fusion
  806.3 0.8 copy.16
  (7 shorter events, 0.0 us)
Async XLA Ops:
  7.2 156.1 %copy-start = (bf16[8192,128]{1,0:T(8,128)(2,1)S(1)}, bf16[8192,128]{1,0:T(8,128)(2,1)}, u32[]{:S(2)}) copy-start(bf16[8192,128]{1,0:T(8,128)(2,1)} %param.10) | copy-start | bytes 6291460
  7.2 156.1 %all-gather.2.cloned.1.call-start = ((), (), s32[]{:S(2)}) async-start(), calls=%async_computation.2 | async-start | bytes 8519680 | tf_op jit(solution)/shard_map/all_gather | solution.py:60
  7.9 389.2 %reduce-scatter.3.cloned.1.call-start = ((), (), s32[]{:S(2)}) async-start(), calls=%async_computation.3 | async-start | bytes 5242880 | tf_op jit(solution)/shard_map/reduce_scatter | solution.py:78
  14.1 334.4 %copy-start.3 = (f32[512]{0:T(512)S(1)}, f32[512]{0:T(512)}, u32[]{:S(2)}) copy-start(f32[512]{0:T(512)} %param.11) | copy-start | bytes 6148
  14.1 334.4 %copy-start.4 = (f32[20]{0:T(128)S(1)}, f32[20]{0:T(128)}, u32[]{:S(2)}) copy-start(f32[20]{0:T(128)} %constant.32.clone) | copy-start | bytes 244
  14.1 334.4 %copy-start.5 = (f32[20]{0:T(128)S(1)}, f32[20]{0:T(128)}, u32[]{:S(2)}) copy-start(f32[20]{0:T(128)} %constant.31.clone) | copy-start | bytes 244
  356.7 448.5 %reduce-scatter.5.cloned.1.call-start = ((), (), s32[]{:S(2)}) async-start(), calls=%async_computation.4 | async-start | bytes 17039360 | tf_op jit(solution)/shard_map/reduce_scatter | solution.py:86
  365.5 0.9 copy-start.1
  365.5 439.7 %copy-start.2 = (f32[128]{0:T(128)S(1)}, f32[128]{0:T(128)}, u32[]{:S(2)}) copy-start(f32[128]{0:T(128)} %param.9) | copy-start | bytes 1540
Sparse Core Ops, SparseCore 0:
  11.5 151.7 all-gather.1
  356.9 40.1 reduce-scatter.2
  399.8 405.3 reduce-scatter.4
where the time goes:
time: 814 us
  waiting for transfers between devices  579 us (71%)
  blocking collectives  187 us (23%)
  matrix products  22.8 us (3%)
  between operations  13.8 us (2%)
    reduce_scatter x1, waiting for transfers between devices, on_device(): lax.psum_scatter(jnp.dot(root, weighted, preferred_element_type=jnp.float...  406 us
    psum x1, blocking collectives, on_device(): post_mean, square_sum = lax.psum((partial_mean, squares), 'col')  180 us
    all_gather x1, waiting for transfers between devices, on_device(): whole = lax.all_gather(proj, 'col', axis=0, tiled=True)  149 us
    reduce_scatter x1, waiting for transfers between devices, on_device(): lax.psum_scatter(lax.dot_general(whole, weighted, (((1,), (1,)), ((), ())...  23.8 us
  transfers between devices with their start and end apart: 3, of which 3 were waited for; matrix products, arithmetic and copies ran while one was open for 2% of the time, Pallas kernels for 0%

commit v1 on v0

v1 whole, which is shorter than its diff:
```python
import functools

import jax
import jax.numpy as jnp
import numpy as np
from jax import lax
from jax.experimental import pallas as pl
from jax.experimental.pallas import tpu as pltpu
from jax.sharding import PartitionSpec as P

WINDOW = 65536
ROWS = 2048
MESH = pl.DeviceIdType.MESH
F32 = jnp.float32
BF16 = jnp.bfloat16
HIGHEST = lax.Precision.HIGHEST

freedom = 4.0
half_knots = [
    0.2453407083009012,
    0.7374737285453944,
    1.234076215395323,
    1.7385377121165861,
    2.2549740020892757,
    2.7888060584281305,
    3.3478545673832163,
    3.944764040115625,
    4.603682449550744,
    5.387480890011233,
]
half_weights = [
    0.4622436696006101,
    0.2866755053628341,
    0.1090172060200233,
    0.024810520887463612,
    0.0032437733422378567,
    0.00022833863601635319,
    7.802556478532063e-06,
    1.0860693707692819e-07,
    4.3993409922731804e-10,
    2.2293936455341508e-13,
]


def slopes(observed, post_mean, post_var):
    knots = [-k for k in half_knots[::-1]] + half_knots
    weights = half_weights[::-1] + half_weights
    spread_root = jnp.sqrt(2.0 * post_var)
    total_mean = jnp.zeros_like(observed)
    total_var = jnp.zeros_like(observed)
    for knot, weight in zip(knots, weights):
        knot = float(np.float32(knot))
        weight = float(np.float32(weight / np.sqrt(np.pi)))
        gap = observed - (post_mean + spread_root * knot)
        term = weight * ((freedom + 1.0) * gap / (freedom + gap * gap))
        total_mean = total_mean + term
        total_var = total_var + term * knot
    factor = WINDOW / ROWS
    return factor * total_mean, factor * total_var / spread_root


def kernel(
    proj, mean, root, resid, table, index,
    out_mean, out_root, out_proj,
    rootb, projb, lat_out, lat_in, wb, grp, grc, gin, gpo, gpi,
    ar_src, ar_z, ar_p_src, ar_p, gm_src, gm_in,
    local_sem, root_ss, root_rs, half_ss, half_rs, z_ss, z_rs,
    lat_ss, lat_rs, az_ss, az_rs, ap_ss, ap_rs, w_ss, w_rs,
    c_ss, c_rs, g_ss, g_rs, gp_ss, gp_rs, gm_ss, gm_rs,
):
    d = lax.axis_index("dp")
    col = lax.axis_index("col")
    xl, core = d // 2, d % 2
    y, z, xh = col // 16, (col // 2) % 8, col % 2
    p = y * 2 + xh
    other = xl * 2 + (1 - core)

    def column(y_, z_, xh_):
        return y_ * 16 + z_ * 2 + xh_

    def p_to(j):
        return ((y + j // 2) % 4) * 2 + (xh + j % 2) % 2

    def p_from(j):
        return ((y + 4 - j // 2) % 4) * 2 + (xh + 2 - j % 2) % 2

    def p_dev(q):
        return (d, column(q // 2, z, q % 2))

    def z_to(j):
        return (z + j) % 8

    def z_from(j):
        return (z + 8 - j) % 8

    def z_dev(q):
        return (d, column(y, q, xh))

    def copy(src, dst, ss, rs, dev):
        return pltpu.make_async_remote_copy(
            src_ref=src, dst_ref=dst, send_sem=ss, recv_sem=rs,
            device_id=dev, device_id_type=MESH,
        )

    def loop(lo, hi, body):
        def step(j, carry):
            body(j)
            return carry
        lax.fori_loop(lo, hi, step, 0)

    to_d = y
    self_gr = to_d == d

    def g_from_dev(s):
        return (s // 2, column(d, z, s % 2))

    barrier = pltpu.get_barrier_semaphore()

    def greet(dev):
        pl.semaphore_signal(barrier, inc=1, device_id=dev, device_id_type=MESH)

    loop(1, 8, lambda j: greet(p_dev(p_from(j))))
    loop(1, 8, lambda j: greet(z_dev(z_from(j))))
    loop(1, 4, lambda j: greet(((d + j) % 4, col)))
    me_gr = d * 2 + xh

    def greet_gr(s):
        @pl.when(jnp.logical_not(jnp.logical_and(self_gr, s == me_gr)))
        def _():
            greet(g_from_dev(s))

    loop(0, 8, greet_gr)
    pl.semaphore_wait(barrier, 7 + 7 + 3 + 8 - jnp.where(self_gr, 1, 0))

    def proj_copy(j, q_to, q_from):
        return copy(proj, projb.at[z], z_ss.at[j], z_rs.at[j], z_dev(q_to))

    def start_z(j):
        copy(proj, projb.at[z], z_ss.at[j], z_rs.at[j], z_dev(z_to(j))).start()

    half = pl.ds(core * 4, 4)

    def cols(q):
        return pl.ds(pl.multiple_of(q * 128, 128), 128)

    def start_root(j):
        q = p_to(j)
        copy(
            root.at[q // 2, half, q % 2], rootb.at[half, :, cols(p)],
            root_ss.at[j], root_rs.at[j], p_dev(q),
        ).start()

    loop(1, 8, start_z)
    loop(1, 8, start_root)
    own_root = pltpu.make_async_copy(root.at[y, half, xh], rootb.at[half, :, cols(p)], local_sem)
    own_root.start()
    projb[z] = proj[...]

    mean_rows = jnp.broadcast_to(mean[...], (8, 128))
    part_mean = jnp.dot(
        mean_rows, proj[...].astype(F32), precision=HIGHEST, preferred_element_type=F32
    )
    ar_src[:, 512:] = part_mean[0:1]
    picked = []
    for part in range(4):
        idx = index[:, part * 128 : (part + 1) * 128]
        row, lane = idx // 128, idx % 128
        chosen = jnp.where(lax.broadcasted_iota(jnp.int32, (512, 128), 0) == row, 1.0, 0.0)
        values = lax.dot_general(
            table[...], chosen, (((0,), (0,)), ((), ())),
            precision=HIGHEST, preferred_element_type=F32,
        )
        here = lax.broadcasted_iota(jnp.int32, (128, 128), 0) == lane
        picked.append(jnp.sum(jnp.where(here, values, 0.0), axis=0, keepdims=True))
    observed = jnp.concatenate(picked, axis=1)

    own_root.wait()

    def wait_root(j):
        q = p_from(j)
        copy(
            root.at[y, half, xh], rootb.at[half, :, cols(q)],
            root_ss.at[j], root_rs.at[j], p_dev(q),
        ).wait_recv()

    loop(1, 8, wait_root)
    share = copy(rootb.at[half], rootb.at[half], half_ss, half_rs, (other, col))
    share.start()

    def wait_z(j):
        q = z_from(j)
        copy(proj, projb.at[q], z_ss.at[j], z_rs.at[j], z_dev(q)).wait_recv()

    loop(1, 8, wait_z)
    other_half = pl.ds((1 - core) * 4, 4)
    copy(rootb.at[other_half], rootb.at[other_half], half_ss, half_rs, (other, col)).wait_recv()

    def latent_piece(q):
        block = rootb[:, :, cols(q)].reshape(1024, 128)
        return lax.dot_general(
            block, projb[...].reshape(1024, 512), (((0,), (0,)), ((), ())),
            preferred_element_type=F32,
        )

    def lat_copy(j, q, slot):
        return copy(lat_out.at[j], lat_in.at[slot], lat_ss.at[j], lat_rs.at[j], p_dev(q))

    def send_lat(j):
        q = p_to(j)
        lat_out[j] = latent_piece(q)
        lat_copy(j, q, p).start()

    loop(1, 8, send_lat)
    lat_in[p] = latent_piece(p)

    def wait_lat(j):
        q = p_from(j)
        lat_copy(j, q, q).wait_recv()

    loop(1, 8, wait_lat)
    latent = lat_in[0]
    for i in range(1, 8):
        latent = latent + lat_in[i]
    lat_in[0] = latent
    ar_src[:, :512] = jnp.sum(latent * latent, axis=0, keepdims=True)

    def az_copy(j, q, slot):
        return copy(ar_src, ar_z.at[slot], az_ss.at[j], az_rs.at[j], z_dev(q))

    loop(1, 8, lambda j: az_copy(j, z_to(j), z).start())
    ar_z[z] = ar_src[...]
    loop(1, 8, lambda j: az_copy(j, z_from(j), z_from(j)).wait_recv())
    total = ar_z[0]
    for i in range(1, 8):
        total = total + ar_z[i]
    ar_p_src[...] = total

    def ap_copy(j, q, slot):
        return copy(ar_p_src, ar_p.at[slot], ap_ss.at[j], ap_rs.at[j], p_dev(q))

    loop(1, 8, lambda j: ap_copy(j, p_to(j), p).start())
    ar_p[p] = total
    loop(1, 8, lambda j: ap_copy(j, p_from(j), p_from(j)).wait_recv())
    total = ar_p[0]
    for i in range(1, 8):
        total = total + ar_p[i]
    post_var = resid[...] + total[:, :512]
    post_mean = total[:, 512:]
    slope_mean, slope_var = slopes(observed, post_mean, post_var)

    wb[p] = (2.0 * slope_var * lat_in[0]).astype(BF16)

    def w_copy(j, q, slot):
        return copy(wb.at[p], wb.at[slot], w_ss.at[j], w_rs.at[j], p_dev(q))

    loop(1, 8, lambda j: w_copy(j, p_to(j), p).start())

    gm = lax.dot_general(
        jnp.broadcast_to(slope_mean, (8, 512)), proj[...].astype(F32),
        (((1,), (1,)), ((), ())), precision=HIGHEST, preferred_element_type=F32,
    )
    gm_src[...] = gm[0:1]
    gm_in[d] = gm[0:1]

    def gm_copy(j, e, slot):
        return copy(gm_src, gm_in.at[slot], gm_ss.at[j], gm_rs.at[j], (e, col))

    loop(1, 4, lambda j: gm_copy(j, (d + j) % 4, d).start())

    own_rows = pl.ds(pl.multiple_of(core * 512, 512), 512)
    other_rows = pl.ds(pl.multiple_of((1 - core) * 512, 512), 512)

    def c_copy(j, q, rows_):
        return copy(grp.at[q, rows_], grc.at[q], c_ss.at[j], c_rs.at[j], (other, col))

    def root_piece(j):
        q = p_from(j)

        @pl.when(j > 0)
        def _():
            w_copy(j, q, q).wait_recv()

        grp[q] = lax.dot_general(
            projb[...].reshape(1024, 512), wb[q], (((1,), (1,)), ((), ())),
            preferred_element_type=F32,
        )
        c_copy(j, q, other_rows).start()

    loop(0, 8, root_piece)

    def gp_copy(j, q, slot):
        return copy(gpo.at[j], gpi.at[slot], gp_ss.at[j], gp_rs.at[j], z_dev(q))

    def proj_piece(q):
        return jnp.dot(rootb[q], wb[...].reshape(1024, 512), preferred_element_type=F32)

    def send_gp(j):
        q = z_to(j)
        gpo[j] = proj_piece(q).astype(BF16)
        gp_copy(j, q, z).start()

    loop(1, 8, send_gp)

    def g_copy(j, q):
        return copy(
            grp.at[q, own_rows], gin.at[me_gr], g_ss.at[j], g_rs.at[me_gr],
            (to_d, column(q // 2, z, q % 2)),
        )

    def send_gr(j):
        q = p_from(j)
        c_copy(j, q, other_rows).wait_recv()
        grp[q, own_rows] = grp[q, own_rows] + grc[q]
        mine = jnp.logical_and(self_gr, j == 0)

        @pl.when(mine)
        def _():
            pltpu.make_async_copy(grp.at[q, own_rows], gin.at[me_gr], g_rs.at[me_gr]).start()

        @pl.when(jnp.logical_not(mine))
        def _():
            g_copy(j, q).start()

    loop(0, 8, send_gr)

    own = proj_piece(z) + jnp.transpose(mean_rows)[:, 0:1] * slope_mean
    loop(1, 4, lambda j: gm_copy(j, (d + 4 - j) % 4, (d + 4 - j) % 4).wait_recv())
    out_mean[...] = gm_in[0] + gm_in[1] + gm_in[2] + gm_in[3]

    loop(1, 8, lambda j: gp_copy(j, z_from(j), z_from(j)).wait_recv())
    out_proj[...] = own

    def add_gp(j):
        out_proj[...] += gpi[z_from(j)].astype(F32)

    loop(1, 8, add_gp)

    def wait_gr(s):
        pltpu.make_async_copy(gin.at[s], gin.at[s], g_rs.at[s]).wait()

    loop(0, 8, wait_gr)
    for k in range(2):
        for h in range(2):
            block = gin[k * 2 + h] + gin[4 + k * 2 + h]
            out_root[k * 4 : k * 4 + 4, h] = block.reshape(4, 128, 128)

    def drain(j):
        z_copy = copy(proj, projb.at[z], z_ss.at[j], z_rs.at[j], z_dev(z_to(j)))
        z_copy.wait_send()
        q = p_to(j)
        copy(
            root.at[q // 2, half, q % 2], rootb.at[half, :, cols(p)],
            root_ss.at[j], root_rs.at[j], p_dev(q),
        ).wait_send()
        lat_copy(j, q, p).wait_send()
        az_copy(j, z_to(j), z).wait_send()
        ap_copy(j, q, p).wait_send()
        w_copy(j, q, p).wait_send()
        gp_copy(j, z_to(j), z).wait_send()

    loop(1, 8, drain)
    share.wait_send()
    loop(1, 4, lambda j: gm_copy(j, (d + j) % 4, d).wait_send())

    def drain_gr(j):
        q = p_from(j)
        c_copy(j, q, other_rows).wait_send()

        @pl.when(jnp.logical_not(jnp.logical_and(self_gr, j == 0)))
        def _():
            g_copy(j, q).wait_send()

    loop(0, 8, drain_gr)


def on_device(proj, mean, root, resid_var, targets, indices):
    vmem = pl.BlockSpec(memory_space=pltpu.VMEM)
    sem = pltpu.SemaphoreType.DMA
    out_mean, out_root, out_proj = pl.pallas_call(
        kernel,
        out_shape=(
            jax.ShapeDtypeStruct((1, 128), F32),
            jax.ShapeDtypeStruct((8, 2, 128, 128), F32),
            jax.ShapeDtypeStruct((128, 512), F32),
        ),
        in_specs=[vmem, vmem, pl.BlockSpec(memory_space=pl.ANY), vmem, vmem, vmem],
        out_specs=(vmem, vmem, vmem),
        scratch_shapes=[
            pltpu.VMEM((8, 128, 1024), BF16),
            pltpu.VMEM((8, 128, 512), BF16),
            pltpu.VMEM((8, 128, 512), F32),
            pltpu.VMEM((8, 128, 512), F32),
            pltpu.VMEM((8, 128, 512), BF16),
            pltpu.VMEM((8, 1024, 128), F32),
            pltpu.VMEM((8, 512, 128), F32),
            pltpu.VMEM((8, 512, 128), F32),
            pltpu.VMEM((8, 128, 512), BF16),
            pltpu.VMEM((8, 128, 512), BF16),
            pltpu.VMEM((1, 1024), F32),
            pltpu.VMEM((8, 1, 1024), F32),
            pltpu.VMEM((1, 1024), F32),
            pltpu.VMEM((8, 1, 1024), F32),
            pltpu.VMEM((1, 128), F32),
            pltpu.VMEM((4, 1, 128), F32),
            sem,
            sem((8,)), sem((8,)), sem, sem, sem((8,)), sem((8,)),
            sem((8,)), sem((8,)), sem((8,)), sem((8,)), sem((8,)), sem((8,)),
            sem((8,)), sem((8,)),
            sem((8,)), sem((8,)), sem((8,)), sem((8,)), sem((8,)), sem((8,)),
            sem((4,)), sem((4,)),
        ],
        compiler_params=pltpu.CompilerParams(
            collective_id=0, has_side_effects=True, vmem_limit_bytes=48 * 2**20
        ),
    )(
        proj,
        mean.reshape(1, 128),
        root.reshape(4, 8, 2, 128, 128),
        resid_var.reshape(1, 512),
        targets.reshape(512, 128),
        indices.reshape(1, 512),
    )
    return out_mean.reshape(128), out_root.reshape(2048, 128), out_proj


def solution(mesh):
    return jax.shard_map(
        on_device,
        mesh=mesh,
        in_specs=(P("col", "dp"), P("col"), P(None, "col"), P("dp"), P(), P("dp")),
        out_specs=(P("col"), P("dp", "col"), P("col", "dp")),
        check_vma=False,
    )
```

time: 814 us -> 141 us (0.17)
  the two profiles are of different devices: /device:TPU:0 before, /device:TPU:7 now
where the time goes in v1:
time: 141 us; the launch traced here: 140 us
  Pallas kernels  132 us (94%)
  local copies, waits for them, and re-layouts  7.64 us (5%)
    pallas_call x1, Pallas kernels, on_device(): pl.pallas_call(kernel, out_shape=(jax.ShapeDtypeStruct((1, 128), F32), ja...  132 us
    unnamed x15, local copies, waits for them, and re-layouts  7.64 us

profile of v1, /device:TPU:7, one launch (start us, length us, event | category | flops | bytes accessed | tf_op | source)
XLA Modules:
  0.0 140.0 jit_solution(2643156812916275345)
XLA Ops:
  0.6 0.0 copy-start
  0.6 1.6 %copy-done = bf16[8192,128]{1,0:T(8,128)(2,1)S(1)} copy-done((bf16[8192,128]{1,0:T(8,128)(2,1)S(1)}, bf16[8192,128]{1,0:T(8,128)(2,1)}, u32[]{:S(2)}) %copy-start) | copy-done | bytes 2097176
  2.2 0.0 copy-start.1
  2.2 0.9 copy-done.1
  3.2 0.0 copy-start.2
  3.2 0.9 copy-done.2
  4.1 0.0 copy-start.3
  4.1 0.7 copy-done.3
  4.8 0.0 copy-start.4
  4.8 0.7 copy-done.4
  5.4 0.0 copy-start.5
  5.4 0.7 copy-done.5
  6.1 131.7 %shard_map.85 = (f32[1,128]{1,0:T(1,128)S(1)}, f32[8,2,128,128]{3,2,1,0:T(8,128)S(1)}, f32[128,512]{1,0:T(8,128)S(1)}) custom-call(bf16[128,512]{1,0:T(8,128)(2,1)S(1)} %copy-done.2, f32[1,128]{1,0:T(1,128)S(1)} %bitcast.12, bf16[4,8,2,128,128]{4,3,2,1,0:T(8,128)(2,1)S(1)} %bitcast.7, f32[1,512]{1,0:T(1,128)S(1)} %bitcast.10, f32[512,128]{1,0:T(8,128)S(1)} %bitcast.9, ...), custom_call_target="tpu_custom_call" | custom-call | tf_op jit(solution)/shard_map/pallas_call | solution.py:379
  137.8 0.5 copy.12
  138.4 1.0 copy.13
  139.3 0.7 copy.14
Async XLA Ops:
  0.6 1.6 %copy-start = (bf16[8192,128]{1,0:T(8,128)(2,1)S(1)}, bf16[8192,128]{1,0:T(8,128)(2,1)}, u32[]{:S(2)}) copy-start(bf16[8192,128]{1,0:T(8,128)(2,1)} %param.8) | copy-start | bytes 6291460
  2.2 0.9 copy-start.1
  3.2 0.9 copy-start.2
  4.1 0.7 copy-start.3
  4.8 0.7 copy-start.4
  5.4 0.7 copy-start.5

commit v2 on v1

v2 whole, which is shorter than its diff:
```python
import functools

import jax
import jax.numpy as jnp
import numpy as np
from jax import lax
from jax.experimental import pallas as pl
from jax.experimental.pallas import tpu as pltpu
from jax.sharding import PartitionSpec as P

WINDOW = 65536
ROWS = 2048
MESH = pl.DeviceIdType.MESH
NH = 2
N = 512 // NH
F32 = jnp.float32
BF16 = jnp.bfloat16
HIGHEST = lax.Precision.HIGHEST

freedom = 4.0
half_knots = [
    0.2453407083009012,
    0.7374737285453944,
    1.234076215395323,
    1.7385377121165861,
    2.2549740020892757,
    2.7888060584281305,
    3.3478545673832163,
    3.944764040115625,
    4.603682449550744,
    5.387480890011233,
]
half_weights = [
    0.4622436696006101,
    0.2866755053628341,
    0.1090172060200233,
    0.024810520887463612,
    0.0032437733422378567,
    0.00022833863601635319,
    7.802556478532063e-06,
    1.0860693707692819e-07,
    4.3993409922731804e-10,
    2.2293936455341508e-13,
]


def slopes(observed, post_mean, post_var):
    knots = [-k for k in half_knots[::-1]] + half_knots
    weights = half_weights[::-1] + half_weights
    spread_root = jnp.sqrt(2.0 * post_var)
    total_mean = jnp.zeros_like(observed)
    total_var = jnp.zeros_like(observed)
    for knot, weight in zip(knots, weights):
        knot = float(np.float32(knot))
        weight = float(np.float32(weight / np.sqrt(np.pi)))
        gap = observed - (post_mean + spread_root * knot)
        term = weight * ((freedom + 1.0) * gap / (freedom + gap * gap))
        total_mean = total_mean + term
        total_var = total_var + term * knot
    factor = WINDOW / ROWS
    return factor * total_mean, factor * total_var / spread_root


def kernel(
    proj_hbm, mean_hbm, root, resid_hbm, table_hbm, index_hbm,
    out_mean, out_root, out_proj,
    proj, mean, resid, table, index, in_sem,
    rootb, projb, lat_out, lat_in, wb, grp, grc, gout, gin, gpo, gpi,
    ar_src, ar_z, ar_p_src, ar_p, gm_src, gm_in,
    local_sem, root_ss, root_rs, half_ss, half_rs, z_ss, z_rs,
    lat_ss, lat_rs, az_ss, az_rs, ap_ss, ap_rs, w_ss, w_rs,
    c_ss, c_rs, g_ss, g_rs, gp_ss, gp_rs, gm_ss, gm_rs,
):
    d = lax.axis_index("dp")
    col = lax.axis_index("col")
    core = d % 2
    y, z, xh = col // 16, (col // 2) % 8, col % 2
    p = y * 2 + xh
    other = d + 1 - 2 * core

    def column(y_, z_, xh_):
        return y_ * 16 + z_ * 2 + xh_

    def p_to(j):
        return ((y + j // 2) % 4) * 2 + (xh + j % 2) % 2

    def p_from(j):
        return ((y + 4 - j // 2) % 4) * 2 + (xh + 2 - j % 2) % 2

    def p_dev(q):
        return (d, column(q // 2, z, q % 2))

    def z_to(j):
        return (z + j) % 8

    def z_from(j):
        return (z + 8 - j) % 8

    def z_dev(q):
        return (d, column(y, q, xh))

    def copy(src, dst, ss, rs, dev):
        return pltpu.make_async_remote_copy(
            src_ref=src, dst_ref=dst, send_sem=ss, recv_sem=rs,
            device_id=dev, device_id_type=MESH,
        )

    def loop(lo, hi, body):
        def step(j, carry):
            body(j)
            return carry
        lax.fori_loop(lo, hi, step, 0)

    incoming = [
        pltpu.make_async_copy(a, b, in_sem.at[i])
        for i, (a, b) in enumerate(
            [
                (proj_hbm, proj), (mean_hbm, mean), (index_hbm, index),
                (table_hbm, table), (resid_hbm, resid),
            ]
        )
    ]
    for item in incoming:
        item.start()

    def cols(q):
        return pl.ds(pl.multiple_of(q * 128, 128), 128)

    own_root = pltpu.make_async_copy(root.at[y, :, xh], rootb.at[:, :, cols(p)], local_sem)
    own_root.start()

    self_gr = y == d
    me_gr = d * 2 + xh

    barrier = pltpu.get_barrier_semaphore()

    def greet(dev):
        pl.semaphore_signal(barrier, inc=1, device_id=dev, device_id_type=MESH)

    greet(z_dev(z_to(1)))
    greet(z_dev(z_from(1)))
    loop(1, 8, lambda j: greet(p_dev(p_from(j))))
    loop(1, 4, lambda j: greet(((d + j) % 4, col)))
    pl.semaphore_wait(barrier, 2 + 7 + 3)

    def part(zz, c):
        if NH == 2:
            return projb.at[c, zz]
        return projb.at[0, zz, :, c * 256 : (c + 1) * 256]

    def ring(way, step, c):
        zz = (z + 8 - way * (step - 1)) % 8
        src = proj.at[:, c * 256 : (c + 1) * 256] if step == 1 else part(zz, c)
        i = (0 if way == 1 else 1) * 2 + c
        return copy(src, part(zz, c), z_ss.at[i, step], z_rs.at[i, step], z_dev((z + 8 + way) % 8))

    def ring_wait(way, step, c):
        zz = (z + 8 - way * step) % 8
        i = (0 if way == 1 else 1) * 2 + c
        copy(part(zz, c), part(zz, c), z_ss.at[i, step], z_rs.at[i, step], z_dev((z + 8 + way) % 8)).wait_recv()

    def goes(way, step, c):
        return step < 4 or (c == 0) == (way == 1)

    half = pl.ds(core * 4, 4)
    other_half = pl.ds((1 - core) * 4, 4)

    def root_copy(j):
        q = p_to(j)
        return copy(
            root.at[q // 2, half, q % 2], rootb.at[half, :, cols(p)],
            root_ss.at[j], root_rs.at[j], p_dev(q),
        )

    incoming[0].wait()
    for c in range(2):
        for way in (1, -1):
            ring(way, 1, c).start()
    loop(1, 8, lambda j: root_copy(j).start())
    for h in range(NH):
        projb[h, z] = proj[:, h * N : (h + 1) * N]
    for item in incoming[1:]:
        item.wait()

    mean_rows = jnp.broadcast_to(mean[...], (8, 128))
    part_mean = jnp.dot(
        mean_rows, proj[...].astype(F32), precision=HIGHEST, preferred_element_type=F32
    )
    for h in range(NH):
        ar_src[h, :, N:] = part_mean[0:1, h * N : (h + 1) * N]
    picked = []
    for i in range(4):
        idx = index[:, i * 128 : (i + 1) * 128]
        row, lane = idx // 128, idx % 128
        chosen = jnp.where(lax.broadcasted_iota(jnp.int32, (512, 128), 0) == row, 1.0, 0.0)
        values = lax.dot_general(
            table[...], chosen, (((0,), (0,)), ((), ())),
            precision=HIGHEST, preferred_element_type=F32,
        )
        here = lax.broadcasted_iota(jnp.int32, (128, 128), 0) == lane
        picked.append(jnp.sum(jnp.where(here, values, 0.0), axis=0, keepdims=True))
    observed = jnp.concatenate(picked, axis=1)

    for step in range(2, 5):
        for c in range(2):
            for way in (1, -1):
                ring_wait(way, step - 1, c)
                if goes(way, step, c):
                    ring(way, step, c).start()

    def share_root(j):
        q = p_from(j)
        copy(
            root.at[y, half, xh], rootb.at[half, :, cols(q)],
            root_ss.at[j], root_rs.at[j], p_dev(q),
        ).wait_recv()
        share_copy(j, half).start()

    def share_copy(j, rows_):
        block = rootb.at[rows_, :, cols(p_from(j))]
        return copy(block, block, half_ss.at[j], half_rs.at[j], (other, col))

    loop(1, 8, share_root)
    ring_wait(1, 4, 0)
    ring_wait(-1, 4, 1)
    own_root.wait()
    loop(1, 8, lambda j: share_copy(j, other_half).wait_recv())

    def latent_piece(h, q):
        block = rootb[:, :, cols(q)].reshape(1024, 128)
        return lax.dot_general(
            block, projb[h].reshape(1024, N), (((0,), (0,)), ((), ())),
            preferred_element_type=F32,
        )

    def lat_copy(h, j, q, slot):
        return copy(
            lat_out.at[h, j], lat_in.at[h, slot], lat_ss.at[h, j], lat_rs.at[h, j], p_dev(q)
        )

    def send_latent(h):
        def body(j):
            q = p_to(j)
            lat_out[h, j] = latent_piece(h, q)
            lat_copy(h, j, q, p).start()

        loop(1, 8, body)
        lat_in[h, p] = latent_piece(h, p)

    def az_copy(h, j, q, slot):
        return copy(ar_src.at[h], ar_z.at[h, slot], az_ss.at[h, j], az_rs.at[h, j], z_dev(q))

    def ap_copy(h, j, q, slot):
        return copy(ar_p_src.at[h], ar_p.at[h, slot], ap_ss.at[h, j], ap_rs.at[h, j], p_dev(q))

    def sum_latent(h):
        def body(j):
            q = p_from(j)
            lat_copy(h, j, q, q).wait_recv()

        loop(1, 8, body)
        latent = lat_in[h, 0]
        for i in range(1, 8):
            latent = latent + lat_in[h, i]
        lat_in[h, 0] = latent
        ar_src[h, :, :N] = jnp.sum(latent * latent, axis=0, keepdims=True)
        loop(1, 8, lambda j: az_copy(h, j, z_to(j), z).start())
        ar_z[h, z] = ar_src[h]

    def sum_along_z(h):
        loop(1, 8, lambda j: az_copy(h, j, z_from(j), z_from(j)).wait_recv())
        total = ar_z[h, 0]
        for i in range(1, 8):
            total = total + ar_z[h, i]
        ar_p_src[h] = total
        loop(1, 8, lambda j: ap_copy(h, j, p_to(j), p).start())
        ar_p[h, p] = total

    def w_copy(h, j, q, slot):
        return copy(wb.at[h, p], wb.at[h, slot], w_ss.at[h, j], w_rs.at[h, j], p_dev(q))

    def send_weighted(h):
        loop(1, 8, lambda j: ap_copy(h, j, p_from(j), p_from(j)).wait_recv())
        total = ar_p[h, 0]
        for i in range(1, 8):
            total = total + ar_p[h, i]
        rows_ = slice(h * N, (h + 1) * N)
        post_var = resid[:, rows_] + total[:, :N]
        slope_mean, slope_var = slopes(observed[:, rows_], total[:, N:], post_var)
        wb[h, p] = (2.0 * slope_var * lat_in[h, 0]).astype(BF16)
        loop(1, 8, lambda j: w_copy(h, j, p_to(j), p).start())
        return slope_mean

    own_rows = pl.ds(pl.multiple_of(core * 512, 512), 512)
    other_rows = pl.ds(pl.multiple_of((1 - core) * 512, 512), 512)

    def c_copy(j, q, rows_):
        return copy(grp.at[q, rows_], grc.at[q], c_ss.at[j], c_rs.at[j], (other, col))

    def root_pieces(h):
        def body(j):
            q = p_from(j)

            @pl.when(j > 0)
            def _():
                w_copy(h, j, q, q).wait_recv()

            piece = lax.dot_general(
                projb[h].reshape(1024, N), wb[h, q], (((1,), (1,)), ((), ())),
                preferred_element_type=F32,
            )
            if h == 0:
                grp[q] = piece
            else:
                grp[q] += piece
            if h == NH - 1:
                c_copy(j, q, other_rows).start()

        loop(0, 8, body)

    def gp_copy(h, j, q, slot):
        return copy(gpo.at[h, j], gpi.at[h, slot], gp_ss.at[h, j], gp_rs.at[h, j], z_dev(q))

    def proj_piece(h, q):
        return jnp.dot(rootb[q], wb[h].reshape(1024, N), preferred_element_type=F32)

    def proj_pieces(h):
        def body(j):
            q = z_to(j)
            gpo[h, j] = proj_piece(h, q).astype(BF16)
            gp_copy(h, j, q, z).start()

        loop(1, 8, body)

    if NH == 1:
        send_latent(0)
        sum_latent(0)
        sum_along_z(0)
        slope_mean = send_weighted(0)
    else:
        send_latent(0)
        send_latent(1)
        sum_latent(0)
        sum_along_z(0)
        first = send_weighted(0)
        sum_latent(1)
        sum_along_z(1)
        root_pieces(0)
        second = send_weighted(1)
        proj_pieces(0)
        slope_mean = jnp.concatenate([first, second], axis=1)

    gm = lax.dot_general(
        jnp.broadcast_to(slope_mean, (8, 512)), proj[...].astype(F32),
        (((1,), (1,)), ((), ())), precision=HIGHEST, preferred_element_type=F32,
    )
    gm_src[...] = gm[0:1]
    gm_in[d] = gm[0:1]

    def gm_copy(j, e, slot):
        return copy(gm_src, gm_in.at[slot], gm_ss.at[j], gm_rs.at[j], (e, col))

    loop(1, 4, lambda j: gm_copy(j, (d + j) % 4, d).start())
    root_pieces(NH - 1)
    proj_pieces(NH - 1)

    def g_copy(j, q):
        return copy(
            gout.at[q], gin.at[me_gr], g_ss.at[j], g_rs.at[me_gr],
            (y, column(q // 2, z, q % 2)),
        )

    def send_gr(j):
        q = p_from(j)
        c_copy(j, q, other_rows).wait_recv()
        gout[q] = (grp[q, own_rows] + grc[q]).astype(BF16)
        mine = jnp.logical_and(self_gr, j == 0)

        @pl.when(mine)
        def _():
            pltpu.make_async_copy(gout.at[q], gin.at[me_gr], g_rs.at[me_gr]).start()

        @pl.when(jnp.logical_not(mine))
        def _():
            g_copy(j, q).start()

    loop(0, 8, send_gr)

    outer = jnp.transpose(mean_rows)[:, 0:1] * slope_mean
    for h in range(NH):
        lat_in[h, 1] = proj_piece(h, z) + outer[:, h * N : (h + 1) * N]
    loop(1, 4, lambda j: gm_copy(j, (d + 4 - j) % 4, (d + 4 - j) % 4).wait_recv())
    out_mean[...] = gm_in[0] + gm_in[1] + gm_in[2] + gm_in[3]

    for h in range(NH):

        def add_gp(j):
            q = z_from(j)
            gp_copy(h, j, q, q).wait_recv()
            lat_in[h, 1] += gpi[h, q].astype(F32)

        loop(1, 8, add_gp)
        out_proj[:, h * N : (h + 1) * N] = lat_in[h, 1]

    def wait_gr(s):
        pltpu.make_async_copy(gin.at[s], gin.at[s], g_rs.at[s]).wait()

    loop(0, 8, wait_gr)
    for k in range(2):
        for h in range(2):
            block = gin[k * 2 + h].astype(F32) + gin[4 + k * 2 + h].astype(F32)
            out_root[k * 4 : k * 4 + 4, h] = block.reshape(4, 128, 128)

    for step in range(1, 5):
        for c in range(2):
            for way in (1, -1):
                if goes(way, step, c):
                    ring(way, step, c).wait_send()

    def drain(j):
        root_copy(j).wait_send()
        share_copy(j, half).wait_send()
        for h in range(NH):
            lat_copy(h, j, p_to(j), p).wait_send()
            az_copy(h, j, z_to(j), z).wait_send()
            ap_copy(h, j, p_to(j), p).wait_send()
            w_copy(h, j, p_to(j), p).wait_send()
            gp_copy(h, j, z_to(j), z).wait_send()

    loop(1, 8, drain)
    loop(1, 4, lambda j: gm_copy(j, (d + j) % 4, d).wait_send())

    def drain_gr(j):
        q = p_from(j)
        c_copy(j, q, other_rows).wait_send()

        @pl.when(jnp.logical_not(jnp.logical_and(self_gr, j == 0)))
        def _():
            g_copy(j, q).wait_send()

    loop(0, 8, drain_gr)


def on_device(proj, mean, root, resid_var, targets, indices):
    vmem = pl.BlockSpec(memory_space=pltpu.VMEM)
    hbm = pl.BlockSpec(memory_space=pltpu.HBM)
    sem = pltpu.SemaphoreType.DMA
    out_mean, out_root, out_proj = pl.pallas_call(
        kernel,
        out_shape=(
            jax.ShapeDtypeStruct((1, 128), F32),
            jax.ShapeDtypeStruct((8, 2, 128, 128), F32),
            jax.ShapeDtypeStruct((128, 512), F32),
        ),
        in_specs=[hbm] * 6,
        out_specs=(vmem, vmem, vmem),
        scratch_shapes=[
            pltpu.VMEM((128, 512), BF16),
            pltpu.VMEM((1, 128), F32),
            pltpu.VMEM((1, 512), F32),
            pltpu.VMEM((512, 128), F32),
            pltpu.VMEM((1, 512), jnp.int32),
            sem((5,)),
            pltpu.VMEM((8, 128, 1024), BF16),
            pltpu.VMEM((NH, 8, 128, N), BF16),
            pltpu.VMEM((NH, 8, 128, N), F32),
            pltpu.VMEM((NH, 8, 128, N), F32),
            pltpu.VMEM((NH, 8, 128, N), BF16),
            pltpu.VMEM((8, 1024, 128), F32),
            pltpu.VMEM((8, 512, 128), F32),
            pltpu.VMEM((8, 512, 128), BF16),
            pltpu.VMEM((8, 512, 128), BF16),
            pltpu.VMEM((NH, 8, 128, N), BF16),
            pltpu.VMEM((NH, 8, 128, N), BF16),
            pltpu.VMEM((NH, 1, 2 * N), F32),
            pltpu.VMEM((NH, 8, 1, 2 * N), F32),
            pltpu.VMEM((NH, 1, 2 * N), F32),
            pltpu.VMEM((NH, 8, 1, 2 * N), F32),
            pltpu.VMEM((1, 128), F32),
            pltpu.VMEM((4, 1, 128), F32),
            sem,
            sem((8,)), sem((8,)), sem((8,)), sem((8,)),
            sem((4, 5)), sem((4, 5)),
            sem((NH, 8)), sem((NH, 8)), sem((NH, 8)), sem((NH, 8)),
            sem((NH, 8)), sem((NH, 8)), sem((NH, 8)), sem((NH, 8)),
            sem((8,)), sem((8,)), sem((8,)), sem((8,)),
            sem((NH, 8)), sem((NH, 8)), sem((4,)), sem((4,)),
        ],
        compiler_params=pltpu.CompilerParams(
            collective_id=0, has_side_effects=True, vmem_limit_bytes=62 * 2**20
        ),
    )(
        proj,
        mean.reshape(1, 128),
        root.reshape(4, 8, 2, 128, 128),
        resid_var.reshape(1, 512),
        targets.reshape(512, 128),
        indices.reshape(1, 512),
    )
    return out_mean.reshape(128), out_root.reshape(2048, 128), out_proj


def solution(mesh):
    return jax.shard_map(
        on_device,
        mesh=mesh,
        in_specs=(P("col", "dp"), P("col"), P(None, "col"), P("dp"), P(), P("dp")),
        out_specs=(P("col"), P("dp", "col"), P("col", "dp")),
        check_vma=False,
    )
```

time: 141 us -> 107 us (0.76)
  Pallas kernels: 132 us -> 102 us
  local copies, waits for them, and re-layouts: 7.64 us -> 4.19 us
    pallas_call x1, Pallas kernels: 132 us -> 102 us  [on_device(): pl.pallas_call(kernel, out_shape=(jax.ShapeDtypeStruct((1, 128), F32), ja...]
    unnamed x15 -> x5, local copies, waits for them, and re-layouts: 7.64 us -> 4.19 us
where the time goes in v2:
time: 107 us; the launch traced here: 106 us
  Pallas kernels  102 us (95%)
  local copies, waits for them, and re-layouts  4.19 us (4%)
    pallas_call x1, Pallas kernels, on_device(): pl.pallas_call(kernel, out_shape=(jax.ShapeDtypeStruct((1, 128), F32), ja...  102 us
    unnamed x5, local copies, waits for them, and re-layouts  4.19 us

profile of v2, /device:TPU:7, one launch (start us, length us, event | category | flops | bytes accessed | tf_op | source)
XLA Modules:
  0.0 106.4 jit_solution(633060484432208139)
XLA Ops:
  0.6 101.6 %shard_map.85 = (f32[1,128]{1,0:T(1,128)}, f32[8,2,128,128]{3,2,1,0:T(8,128)}, f32[128,512]{1,0:T(8,128)}) custom-call(bf16[128,512]{1,0:T(8,128)(2,1)} %proj_hbm.1, f32[1,128]{1,0:T(1,128)} %bitcast.12, bf16[4,8,2,128,128]{4,3,2,1,0:T(8,128)(2,1)} %bitcast.7, f32[1,512]{1,0:T(1,128)} %bitcast.10, f32[512,128]{1,0:T(8,128)} %bitcast.9, s32[1,512]{1,0:T(1,128)} %bitcast.11), custom_call_target="tpu_custom_call" | custom-call | tf_op jit(solution)/shard_map/pallas_call | solution.py:448
  102.2 0.0 copy-start
  102.2 1.2 %copy.12 = f32[128]{0:T(128)} copy(f32[128]{0:T(128)} %bitcast.13) | data formatting | bytes 1024
  103.5 2.3 %copy.13 = f32[2048,128]{1,0:T(8,128)} copy(f32[2048,128]{1,0:T(8,128)} %bitcast.8) | data formatting | bytes 2097152
  105.7 0.0 copy-done
  105.7 0.7 copy.14
Async XLA Ops:
  102.2 3.5 %copy-start = (f32[128,512]{1,0:T(8,128)S(1)}, f32[128,512]{1,0:T(8,128)}, u32[]{:S(2)}) copy-start(f32[128,512]{1,0:T(8,128)} %get-tuple-element.14) | copy-start | bytes 786436

commit v3 on v2

--- a/solution.py
+++ b/solution.py
@@ -65,11 +65,11 @@
     proj_hbm, mean_hbm, root, resid_hbm, table_hbm, index_hbm,
     out_mean, out_root, out_proj,
     proj, mean, resid, table, index, in_sem,
-    rootb, projb, lat_out, lat_in, wb, grp, grc, gout, gin, gpo, gpi,
+    rootb, projb, projx, lat_out, lat_in, wb, wx, grp, gout, mid, gin, gpo, gpi,
     ar_src, ar_z, ar_p_src, ar_p, gm_src, gm_in,
     local_sem, root_ss, root_rs, half_ss, half_rs, z_ss, z_rs,
     lat_ss, lat_rs, az_ss, az_rs, ap_ss, ap_rs, w_ss, w_rs,
-    c_ss, c_rs, g_ss, g_rs, gp_ss, gp_rs, gm_ss, gm_rs,
+    px_ss, px_rs, x_ss, x_rs, m_ss, m_rs, g_ss, g_rs, gp_ss, gp_rs, gm_ss, gm_rs,
 ):
     d = lax.axis_index("dp")
     col = lax.axis_index("col")
@@ -129,7 +129,6 @@
     own_root = pltpu.make_async_copy(root.at[y, :, xh], rootb.at[:, :, cols(p)], local_sem)
     own_root.start()
 
-    self_gr = y == d
     me_gr = d * 2 + xh
 
     barrier = pltpu.get_barrier_semaphore()
@@ -137,30 +136,53 @@
     def greet(dev):
         pl.semaphore_signal(barrier, inc=1, device_id=dev, device_id_type=MESH)
 
-    greet(z_dev(z_to(1)))
-    greet(z_dev(z_from(1)))
+    for j in (1, 2):
+        greet(z_dev(z_to(j)))
+        greet(z_dev(z_from(j)))
     loop(1, 8, lambda j: greet(p_dev(p_from(j))))
     loop(1, 4, lambda j: greet(((d + j) % 4, col)))
-    pl.semaphore_wait(barrier, 2 + 7 + 3)
+    pl.semaphore_wait(barrier, 4 + 7 + 3)
 
     def part(zz, c):
         if NH == 2:
             return projb.at[c, zz]
         return projb.at[0, zz, :, c * 256 : (c + 1) * 256]
 
-    def ring(way, step, c):
-        zz = (z + 8 - way * (step - 1)) % 8
-        src = proj.at[:, c * 256 : (c + 1) * 256] if step == 1 else part(zz, c)
+    def first(way, dist, c):
         i = (0 if way == 1 else 1) * 2 + c
-        return copy(src, part(zz, c), z_ss.at[i, step], z_rs.at[i, step], z_dev((z + 8 + way) % 8))
-
-    def ring_wait(way, step, c):
-        zz = (z + 8 - way * step) % 8
+        block = part(z, c)
+        return copy(block, block, z_ss.at[i, dist], z_rs.at[i, dist], z_dev((z + 8 + way * dist) % 8))
+
+    def onward(way, dist, c):
         i = (0 if way == 1 else 1) * 2 + c
-        copy(part(zz, c), part(zz, c), z_ss.at[i, step], z_rs.at[i, step], z_dev((z + 8 + way) % 8)).wait_recv()
-
-    def goes(way, step, c):
-        return step < 4 or (c == 0) == (way == 1)
+        block = part((z + 8 - way * 2) % 8, c)
+        return copy(block, block, z_ss.at[i, dist], z_rs.at[i, dist], z_dev((z + 8 + way * (dist - 2)) % 8))
+
+    def goes(way, dist, c):
+        return dist < 4 or (c == 0) == (way == 1)
+
+    def arrived(way, dist, c):
+        i = (0 if way == 1 else 1) * 2 + c
+        block = part((z + 8 - way * dist) % 8, c)
+        copy(block, block, z_ss.at[i, dist], z_rs.at[i, dist], z_dev((z + 8 + way) % 8)).wait_recv()
+
+    def send_first(c):
+        for dist in (2, 1):
+            for way in (1, -1):
+                first(way, dist, c).start()
+
+    def send_onward(c):
+        for way in (1, -1):
+            arrived(way, 2, c)
+            for dist in (4, 3):
+                if goes(way, dist, c):
+                    onward(way, dist, c).start()
+
+    def all_arrived(c):
+        for dist in (1, 3, 4):
+            for way in (1, -1):
+                if goes(way, dist, c):
+                    arrived(way, dist, c)
 
     half = pl.ds(core * 4, 4)
     other_half = pl.ds((1 - core) * 4, 4)
@@ -173,12 +195,11 @@
         )
 
     incoming[0].wait()
-    for c in range(2):
-        for way in (1, -1):
-            ring(way, 1, c).start()
-    loop(1, 8, lambda j: root_copy(j).start())
     for h in range(NH):
         projb[h, z] = proj[:, h * N : (h + 1) * N]
+    send_first(0)
+    loop(1, 8, lambda j: root_copy(j).start())
+    send_first(1)
     for item in incoming[1:]:
         item.wait()
 
@@ -188,6 +209,7 @@
     )
     for h in range(NH):
         ar_src[h, :, N:] = part_mean[0:1, h * N : (h + 1) * N]
+    send_onward(0)
     picked = []
     for i in range(4):
         idx = index[:, i * 128 : (i + 1) * 128]
@@ -201,12 +223,7 @@
         picked.append(jnp.sum(jnp.where(here, values, 0.0), axis=0, keepdims=True))
     observed = jnp.concatenate(picked, axis=1)
 
-    for step in range(2, 5):
-        for c in range(2):
-            for way in (1, -1):
-                ring_wait(way, step - 1, c)
-                if goes(way, step, c):
-                    ring(way, step, c).start()
+    send_onward(1)
 
     def share_root(j):
         q = p_from(j)
@@ -220,32 +237,46 @@
         block = rootb.at[rows_, :, cols(p_from(j))]
         return copy(block, block, half_ss.at[j], half_rs.at[j], (other, col))
 
-    loop(1, 8, share_root)
-    ring_wait(1, 4, 0)
-    ring_wait(-1, 4, 1)
     own_root.wait()
-    loop(1, 8, lambda j: share_copy(j, other_half).wait_recv())
-
-    def latent_piece(h, q):
-        block = rootb[:, :, cols(q)].reshape(1024, 128)
-        return lax.dot_general(
-            block, projb[h].reshape(1024, N), (((0,), (0,)), ((), ())),
-            preferred_element_type=F32,
-        )
+    all_arrived(0)
 
     def lat_copy(h, j, q, slot):
         return copy(
-            lat_out.at[h, j], lat_in.at[h, slot], lat_ss.at[h, j], lat_rs.at[h, j], p_dev(q)
+            lat_out.at[h, q], lat_in.at[h, slot], lat_ss.at[h, j], lat_rs.at[h, j], p_dev(q)
         )
 
     def send_latent(h):
-        def body(j):
-            q = p_to(j)
-            lat_out[h, j] = latent_piece(h, q)
-            lat_copy(h, j, q, p).start()
-
-        loop(1, 8, body)
-        lat_in[h, p] = latent_piece(h, p)
+        def body(i):
+            pair = (y + 4 - i) % 4
+            if h == 0:
+
+                @pl.when(i > 0)
+                def _():
+                    share_root(2 * i)
+
+                share_root(2 * i + 1)
+
+                @pl.when(i > 0)
+                def _():
+                    share_copy(2 * i, other_half).wait_recv()
+
+                share_copy(2 * i + 1, other_half).wait_recv()
+            block = rootb[:, :, pl.ds(pl.multiple_of(pair * 256, 256), 256)].reshape(1024, 256)
+            piece = lax.dot_general(
+                block, projb[h].reshape(1024, N), (((0,), (0,)), ((), ())),
+                preferred_element_type=F32,
+            )
+            lat_out[h, pl.ds(pair * 2, 2)] = piece.reshape(2, 128, N)
+            ahead = ((4 - i) % 4) * 2
+
+            @pl.when(i > 0)
+            def _():
+                lat_copy(h, ahead, p_to(ahead), p).start()
+
+            lat_copy(h, ahead + 1, p_to(ahead + 1), p).start()
+
+        loop(0, 4, body)
+        lat_in[h, p] = lat_out[h, p]
 
     def az_copy(h, j, q, slot):
         return copy(ar_src.at[h], ar_z.at[h, slot], az_ss.at[h, j], az_rs.at[h, j], z_dev(q))
@@ -291,64 +322,142 @@
         loop(1, 8, lambda j: w_copy(h, j, p_to(j), p).start())
         return slope_mean
 
-    own_rows = pl.ds(pl.multiple_of(core * 512, 512), 512)
-    other_rows = pl.ds(pl.multiple_of((1 - core) * 512, 512), 512)
-
-    def c_copy(j, q, rows_):
-        return copy(grp.at[q, rows_], grc.at[q], c_ss.at[j], c_rs.at[j], (other, col))
-
-    def root_pieces(h):
+    def x_copy(h, j, q):
+        return copy(wb.at[h, q], wx.at[h, q], x_ss.at[h, j], x_rs.at[h, j], (other, col))
+
+    def hand_on(h):
         def body(j):
             q = p_from(j)
-
-            @pl.when(j > 0)
+            w_copy(h, j, q, q).wait_recv()
+            x_copy(h, j, q).start()
+
+        x_copy(h, 0, p).start()
+        loop(1, 8, body)
+
+    def root_pair(h, i):
+        pair = (y + 4 - i) % 4
+        x_copy(h, 2 * i, p_from(2 * i)).wait_recv()
+        x_copy(h, 2 * i + 1, p_from(2 * i + 1)).wait_recv()
+        both = pl.ds(pair * 2, 2)
+        mine = lax.dot_general(
+            projb[h, half].reshape(512, N), wb[h, both].reshape(256, N),
+            (((1,), (1,)), ((), ())), preferred_element_type=F32,
+        )
+        return mine + lax.dot_general(
+            projx[h].reshape(512, N), wx[h, both].reshape(256, N),
+            (((1,), (1,)), ((), ())), preferred_element_type=F32,
+        )
+
+    def root_first():
+        def body(i):
+            grp[i] = root_pair(0, i)
+
+        loop(0, 4, body)
+
+    def m_copy(i, pair, slot):
+        return copy(
+            gout.at[pl.ds(pair * 2, 2)], mid.at[slot], m_ss.at[i], m_rs.at[slot],
+            p_dev(pair * 2 + xh),
+        )
+
+    def root_last():
+        def body(i):
+            piece = root_pair(NH - 1, i)
+            if NH == 2:
+                piece = piece + grp[i]
+            pair = (y + 4 - i) % 4
+            left, right = piece[:, :128].astype(BF16), piece[:, 128:].astype(BF16)
+
+            @pl.when(i > 0)
             def _():
-                w_copy(h, j, q, q).wait_recv()
-
-            piece = lax.dot_general(
-                projb[h].reshape(1024, N), wb[h, q], (((1,), (1,)), ((), ())),
+                gout[pair * 2] = left
+                gout[pair * 2 + 1] = right
+                m_copy(i, pair, y).start()
+
+            @pl.when(i == 0)
+            def _():
+                mid[y, 0] = left
+                mid[y, 1] = right
+
+        loop(0, 4, body)
+
+    def g_copy(ys, b):
+        return copy(
+            mid.at[ys, b], gin.at[me_gr], g_ss.at[ys * 2 + b], g_rs.at[me_gr],
+            (ys, column(y, z, b)),
+        )
+
+    def to_owners():
+        def body(t):
+            ys = (y + t) % 4
+
+            @pl.when(t > 0)
+            def _():
+                m_copy(t, ys, ys).wait_recv()
+
+            for b in range(2):
+                mine = jnp.logical_and(ys == d, xh == b)
+
+                @pl.when(mine)
+                def _():
+                    pltpu.make_async_copy(mid.at[ys, b], gin.at[me_gr], g_rs.at[me_gr]).start()
+
+                @pl.when(jnp.logical_not(mine))
+                def _():
+                    g_copy(ys, b).start()
+
+        loop(0, 4, body)
+
+    def gp_copy(h, j, q, slot):
+        return copy(gpo.at[h, q], gpi.at[h, slot], gp_ss.at[h, j], gp_rs.at[h, j], z_dev(q))
+
+    def proj_pieces(h):
+        def body(i):
+            base = ((z // 4 + 1 + i) % 2) * 4
+            four = pl.ds(base, 4)
+            piece = jnp.dot(
+                rootb[four].reshape(512, 1024), wb[h].reshape(1024, N),
                 preferred_element_type=F32,
             )
-            if h == 0:
-                grp[q] = piece
-            else:
-                grp[q] += piece
-            if h == NH - 1:
-                c_copy(j, q, other_rows).start()
-
-        loop(0, 8, body)
-
-    def gp_copy(h, j, q, slot):
-        return copy(gpo.at[h, j], gpi.at[h, slot], gp_ss.at[h, j], gp_rs.at[h, j], z_dev(q))
+            gpo[h, four] = piece.astype(BF16).reshape(4, 128, N)
+            for k in range(4):
+                q = base + k
+
+                @pl.when(q != z)
+                def _():
+                    gp_copy(h, (q + 8 - z) % 8, q, z).start()
+
+        loop(0, 2, body)
 
     def proj_piece(h, q):
         return jnp.dot(rootb[q], wb[h].reshape(1024, N), preferred_element_type=F32)
 
-    def proj_pieces(h):
-        def body(j):
-            q = z_to(j)
-            gpo[h, j] = proj_piece(h, q).astype(BF16)
-            gp_copy(h, j, q, z).start()
-
-        loop(1, 8, body)
-
     if NH == 1:
+        all_arrived(1)
+        px_copy = copy(projb.at[:, other_half], projx, px_ss, px_rs, (other, col))
+        px_copy.start()
         send_latent(0)
         sum_latent(0)
         sum_along_z(0)
         slope_mean = send_weighted(0)
+        px_copy.wait_recv()
     else:
         send_latent(0)
+        all_arrived(1)
         send_latent(1)
+        px_copy = copy(projb.at[:, other_half], projx, px_ss, px_rs, (other, col))
+        px_copy.start()
         sum_latent(0)
         sum_along_z(0)
-        first = send_weighted(0)
+        early = send_weighted(0)
         sum_latent(1)
         sum_along_z(1)
-        root_pieces(0)
+        hand_on(0)
         second = send_weighted(1)
+        px_copy.wait_recv()
         proj_pieces(0)
-        slope_mean = jnp.concatenate([first, second], axis=1)
+        root_first()
+        slope_mean = jnp.concatenate([early, second], axis=1)
 
     gm = lax.dot_general(
         jnp.broadcast_to(slope_mean, (8, 512)), proj[...].astype(F32),
@@ -361,61 +470,16 @@
         return copy(gm_src, gm_in.at[slot], gm_ss.at[j], gm_rs.at[j], (e, col))
 
     loop(1, 4, lambda j: gm_copy(j, (d + j) % 4, d).start())
-    root_pieces(NH - 1)
+    hand_on(NH - 1)
     proj_pieces(NH - 1)
-
-    def g_copy(j, q):
-        return copy(
-            gout.at[q], gin.at[me_gr], g_ss.at[j], g_rs.at[me_gr],
-            (y, column(q // 2, z, q % 2)),
-        )
-
-    def send_gr(j):
-        q = p_from(j)
-        c_copy(j, q, other_rows).wait_recv()
-        gout[q] = (grp[q, own_rows] + grc[q]).astype(BF16)
-        mine = jnp.logical_and(self_gr, j == 0)
-
-        @pl.when(mine)
-        def _():
-            pltpu.make_async_copy(gout.at[q], gin.at[me_gr], g_rs.at[me_gr]).start()
-
-        @pl.when(jnp.logical_not(mine))
-        def _():
-            g_copy(j, q).start()
-
-    loop(0, 8, send_gr)
-
-    outer = jnp.transpose(mean_rows)[:, 0:1] * slope_mean
-    for h in range(NH):
-        lat_in[h, 1] = proj_piece(h, z) + outer[:, h * N : (h + 1) * N]
-    loop(1, 4, lambda j: gm_copy(j, (d + 4 - j) % 4, (d + 4 - j) % 4).wait_recv())
-    out_mean[...] = gm_in[0] + gm_in[1] + gm_in[2] + gm_in[3]
-
-    for h in range(NH):
-
-        def add_gp(j):
-            q = z_from(j)
-            gp_copy(h, j, q, q).wait_recv()
-            lat_in[h, 1] += gpi[h, q].astype(F32)
-
-        loop(1, 8, add_gp)
-        out_proj[:, h * N : (h + 1) * N] = lat_in[h, 1]
-
-    def wait_gr(s):
-        pltpu.make_async_copy(gin.at[s], gin.at[s], g_rs.at[s]).wait()
-
-    loop(0, 8, wait_gr)
-    for k in range(2):
-        for h in range(2):
-            block = gin[k * 2 + h].astype(F32) + gin[4 + k * 2 + h].astype(F32)
-            out_root[k * 4 : k * 4 + 4, h] = block.reshape(4, 128, 128)
-
-    for step in range(1, 5):
+    root_last()
+    to_owners()
+
+    for way in (1, -1):
         for c in range(2):
-            for way in (1, -1):
-                if goes(way, step, c):
-                    ring(way, step, c).wait_send()
+            for dist in range(1, 5):
+                if goes(way, dist, c):
+                    (first if dist < 3 else onward)(way, dist, c).wait_send()
 
     def drain(j):
         root_copy(j).wait_send()
@@ -425,20 +489,52 @@
             az_copy(h, j, z_to(j), z).wait_send()
             ap_copy(h, j, p_to(j), p).wait_send()
             w_copy(h, j, p_to(j), p).wait_send()
-            gp_copy(h, j, z_to(j), z).wait_send()
+            x_copy(h, j, p_from(j)).wait_send()
 
     loop(1, 8, drain)
     loop(1, 4, lambda j: gm_copy(j, (d + j) % 4, d).wait_send())
 
-    def drain_gr(j):
-        q = p_from(j)
-        c_copy(j, q, other_rows).wait_send()
-
-        @pl.when(jnp.logical_not(jnp.logical_and(self_gr, j == 0)))
-        def _():
-            g_copy(j, q).wait_send()
-
-    loop(0, 8, drain_gr)
+    px_copy.wait_send()
+    for h in range(NH):
+        x_copy(h, 0, p).wait_send()
+
+    outer = jnp.transpose(mean_rows)[:, 0:1] * slope_mean
+    for h in range(NH):
+        lat_in[h, 1] = proj_piece(h, z) + outer[:, h * N : (h + 1) * N]
+    loop(1, 4, lambda j: gm_copy(j, (d + 4 - j) % 4, (d + 4 - j) % 4).wait_recv())
+    out_mean[...] = gm_in[0] + gm_in[1] + gm_in[2] + gm_in[3]
+
+    for h in range(NH):
+
+        def add_gp(j):
+            q = z_from(j)
+            gp_copy(h, j, q, q).wait_recv()
+            lat_in[h, 1] += gpi[h, q].astype(F32)
+
+        loop(1, 8, add_gp)
+        out_proj[:, h * N : (h + 1) * N] = lat_in[h, 1]
+
+    def wait_gr(s):
+        pltpu.make_async_copy(gin.at[s], gin.at[s], g_rs.at[s]).wait()
+
+    loop(0, 8, wait_gr)
+    for k in range(2):
+        for h in range(2):
+            block = gin[k * 2 + h].astype(F32) + gin[4 + k * 2 + h].astype(F32)
+            out_root[k * 4 : k * 4 + 4, h] = block.reshape(4, 128, 128)
+
+    for h in range(NH):
+        loop(1, 8, lambda j: gp_copy(h, j, z_to(j), z).wait_send())
+    loop(1, 4, lambda i: m_copy(i, (y + 4 - i) % 4, y).wait_send())
+
+    def drain_gr(ys):
+        for b in range(2):
+
+            @pl.when(jnp.logical_not(jnp.logical_and(ys == d, xh == b)))
+            def _():
+                g_copy(ys, b).wait_send()
+
+    loop(0, 4, drain_gr)
 
 
 def on_device(proj, mean, root, resid_var, targets, indices):
@@ -463,12 +559,14 @@
             sem((5,)),
             pltpu.VMEM((8, 128, 1024), BF16),
             pltpu.VMEM((NH, 8, 128, N), BF16),
+            pltpu.VMEM((NH, 4, 128, N), BF16),
             pltpu.VMEM((NH, 8, 128, N), F32),
             pltpu.VMEM((NH, 8, 128, N), F32),
             pltpu.VMEM((NH, 8, 128, N), BF16),
-            pltpu.VMEM((8, 1024, 128), F32),
-            pltpu.VMEM((8, 512, 128), F32),
+            pltpu.VMEM((NH, 8, 128, N), BF16),
+            pltpu.VMEM((4, 512, 256), F32),
             pltpu.VMEM((8, 512, 128), BF16),
+            pltpu.VMEM((4, 2, 512, 128), BF16),
             pltpu.VMEM((8, 512, 128), BF16),
             pltpu.VMEM((NH, 8, 128, N), BF16),
             pltpu.VMEM((NH, 8, 128, N), BF16),
@@ -483,7 +581,7 @@
             sem((4, 5)), sem((4, 5)),
             sem((NH, 8)), sem((NH, 8)), sem((NH, 8)), sem((NH, 8)),
             sem((NH, 8)), sem((NH, 8)), sem((NH, 8)), sem((NH, 8)),
-            sem((8,)), sem((8,)), sem((8,)), sem((8,)),
+            sem, sem, sem((NH, 8)), sem((NH, 8)), sem((4,)), sem((4,)), sem((8,)), sem((8,)),
             sem((NH, 8)), sem((NH, 8)), sem((4,)), sem((4,)),
         ],
         compiler_params=pltpu.CompilerParams(

time: 107 us -> 104 us (0.972)
  Pallas kernels: 102 us -> 99.4 us
    pallas_call x1, Pallas kernels: 102 us -> 99.4 us  [on_device(): pl.pallas_call(kernel, out_shape=(jax.ShapeDtypeStruct((1, 128), F32), ja...]
where the time goes in v3:
time: 104 us
  Pallas kernels  99.4 us (96%)
  local copies, waits for them, and re-layouts  4.19 us (4%)
    pallas_call x1, Pallas kernels, on_device(): pl.pallas_call(kernel, out_shape=(jax.ShapeDtypeStruct((1, 128), F32), ja...  99.4 us
    unnamed x5, local copies, waits for them, and re-layouts  4.19 us

profile of v3, /device:TPU:7, one launch (start us, length us, event | category | flops | bytes accessed | tf_op | source)
XLA Modules:
  0.0 104.3 jit_solution(6364299084518838686)
XLA Ops:
  0.6 99.4 %shard_map.85 = (f32[1,128]{1,0:T(1,128)}, f32[8,2,128,128]{3,2,1,0:T(8,128)}, f32[128,512]{1,0:T(8,128)}) custom-call(bf16[128,512]{1,0:T(8,128)(2,1)} %proj_hbm.1, f32[1,128]{1,0:T(1,128)} %bitcast.12, bf16[4,8,2,128,128]{4,3,2,1,0:T(8,128)(2,1)} %bitcast.7, f32[1,512]{1,0:T(1,128)} %bitcast.10, f32[512,128]{1,0:T(8,128)} %bitcast.9, s32[1,512]{1,0:T(1,128)} %bitcast.11), custom_call_target="tpu_custom_call" | custom-call | tf_op jit(solution)/shard_map/pallas_call | solution.py:544
  100.1 0.0 copy-start
  100.1 1.2 %copy.12 = f32[128]{0:T(128)} copy(f32[128]{0:T(128)} %bitcast.13) | data formatting | bytes 1024
  101.3 2.3 %copy.13 = f32[2048,128]{1,0:T(8,128)} copy(f32[2048,128]{1,0:T(8,128)} %bitcast.8) | data formatting | bytes 2097152
  103.6 0.0 copy-done
  103.6 0.7 copy.14
Async XLA Ops:
  100.1 3.5 %copy-start = (f32[128,512]{1,0:T(8,128)S(1)}, f32[128,512]{1,0:T(8,128)}, u32[]{:S(2)}) copy-start(f32[128,512]{1,0:T(8,128)} %get-tuple-element.14) | copy-start | bytes 786436

commit v4 on v3

--- a/solution.py
+++ b/solution.py
@@ -445,15 +445,15 @@
         send_latent(0)
         all_arrived(1)
         send_latent(1)
-        px_copy = copy(projb.at[:, other_half], projx, px_ss, px_rs, (other, col))
-        px_copy.start()
         sum_latent(0)
         sum_along_z(0)
         early = send_weighted(0)
+        px_copy = copy(projb.at[:, other_half], projx, px_ss, px_rs, (other, col))
+        px_copy.start()
         sum_latent(1)
         sum_along_z(1)
+        second = send_weighted(1)
         hand_on(0)
-        second = send_weighted(1)
         px_copy.wait_recv()
         proj_pieces(0)
         root_first()
@@ -518,10 +518,9 @@
         pltpu.make_async_copy(gin.at[s], gin.at[s], g_rs.at[s]).wait()
 
     loop(0, 8, wait_gr)
-    for k in range(2):
-        for h in range(2):
-            block = gin[k * 2 + h].astype(F32) + gin[4 + k * 2 + h].astype(F32)
-            out_root[k * 4 : k * 4 + 4, h] = block.reshape(4, 128, 128)
+    for s_ in range(8):
+        a, k, b = s_ // 4, (s_ // 2) % 2, s_ % 2
+        out_root[a, k * 4 : k * 4 + 4, b] = gin[s_].reshape(4, 128, 128)
 
     for h in range(NH):
         loop(1, 8, lambda j: gp_copy(h, j, z_to(j), z).wait_send())
@@ -545,7 +544,7 @@
         kernel,
         out_shape=(
             jax.ShapeDtypeStruct((1, 128), F32),
-            jax.ShapeDtypeStruct((8, 2, 128, 128), F32),
+            jax.ShapeDtypeStruct((2, 8, 2, 128, 128), BF16),
             jax.ShapeDtypeStruct((128, 512), F32),
         ),
         in_specs=[hbm] * 6,
@@ -595,7 +594,9 @@
         targets.reshape(512, 128),
         indices.reshape(1, 512),
     )
-    return out_mean.reshape(128), out_root.reshape(2048, 128), out_proj
+    shares = out_root.reshape(2, 2048, 128).astype(F32)
+    grad_root = shares[0] + shares[1]
+    return out_mean.reshape(128), grad_root, out_proj
 
 
 def solution(mesh):

time: 104 us -> 104 us (level)
  local copies, waits for them, and re-layouts: 4.19 us -> 1.22 us
  other arithmetic: 0 us -> 2.54 us
    unnamed x5 -> x6, local copies, waits for them, and re-layouts: 4.19 us -> 1.22 us
    convert_element_type x0 -> x1, other arithmetic: none -> 1.45 us  [on_device(): shares = out_root.reshape(2, 2048, 128).astype(F32)]
    add x0 -> x1, other arithmetic: none -> 1.08 us  [on_device(): grad_root = shares[0] + shares[1]]
where the time goes in v4:
time: 104 us
  Pallas kernels  99.4 us (96%)
  other arithmetic  2.54 us (2%)
  local copies, waits for them, and re-layouts  1.22 us (1%)
    pallas_call x1, Pallas kernels, on_device(): pl.pallas_call(kernel, out_shape=(jax.ShapeDtypeStruct((1, 128), F32), ja...  99.4 us

profile of v4, /device:TPU:7, one launch (start us, length us, event | category | flops | bytes accessed | tf_op | source)
XLA Modules:
  0.0 103.8 jit_solution(8926370228415142426)
XLA Ops:
  0.6 99.4 %shard_map.85 = (f32[1,128]{1,0:T(1,128)}, bf16[2,8,2,128,128]{4,3,2,1,0:T(8,128)(2,1)}, f32[128,512]{1,0:T(8,128)}) custom-call(bf16[128,512]{1,0:T(8,128)(2,1)} %proj_hbm.1, f32[1,128]{1,0:T(1,128)} %bitcast.12, bf16[4,8,2,128,128]{4,3,2,1,0:T(8,128)(2,1)} %bitcast.7, f32[1,512]{1,0:T(1,128)} %bitcast.10, f32[512,128]{1,0:T(8,128)} %bitcast.9, ...), custom_call_target="tpu_custom_call" | custom-call | tf_op jit(solution)/shard_map/pallas_call | solution.py:543
  100.0 1.5 %convert_element_type.4 = f32[2,8,2,128,128]{4,3,2,1,0:T(8,128)S(1)} convert(bf16[2,8,2,128,128]{4,3,2,1,0:T(8,128)(2,1)} %get-tuple-element.7) | non-fusion elementwise | flops 524288 | bytes 3145728 | tf_op jit(solution)/shard_map/convert_element_type | solution.py:597
  101.5 0.0 copy-start.1
  101.5 0.0 copy-start
  101.5 1.1 %slice_add_fusion = f32[1,8,2,128,128]{4,3,2,1,0:T(8,128)} fusion(f32[2,8,2,128,128]{4,3,2,1,0:T(8,128)S(1)} %convert_element_type.4), kind=kLoop, calls=%fused_computation | loop fusion | flops 262144 | bytes 3145728 | tf_op jit(solution)/shard_map/add | solution.py:598
  102.6 0.0 copy-done.1
  102.6 0.5 copy.11
  103.1 0.0 copy-done
  103.1 0.7 copy.12
Async XLA Ops:
  101.5 1.1 %copy-start.1 = (f32[1,128]{1,0:T(1,128)S(1)}, f32[1,128]{1,0:T(1,128)}, u32[]{:S(2)}) copy-start(f32[1,128]{1,0:T(1,128)} %get-tuple-element.6) | copy-start | bytes 1540
  101.5 1.6 %copy-start = (f32[128,512]{1,0:T(8,128)S(1)}, f32[128,512]{1,0:T(8,128)}, u32[]{:S(2)}) copy-start(f32[128,512]{1,0:T(8,128)} %get-tuple-element.14) | copy-start | bytes 786436
